TPU v7x, 32 devices: a whole 2x2x4 slice. The times are simulated.
32 devices in a mesh: feat: 16 (over z, x, core), dp: 2 (over y).
Axes of the slice: x: 2, y: 2, z: 4, core: 2. Of those that a mesh axis runs over, the one named last changes fastest.
Arguments:
- x_feat: bfloat16 [2, 1024, 26624], P('dp', 'feat'), may hold values from -6 to 6
- tiles_one: bfloat16 [2, 64, 128, 128], P('dp', 'feat'), may hold values from 0 to 0.13183594
- tile_cols: int32 [2, 64], P('dp', 'feat'), may hold values from 0 to 207
- tile_counts: int32 [2, 16], P('dp', 'feat'), may hold values from 1 to 4, as said below
- w_one: bfloat16 [2, 1024, 256], P(None, 'feat'), may hold values from -0.1875 to 0.1875
- b_one: float32 [256], replicated, may hold values from -3 to 3
- adj_two: bfloat16 [2, 2048, 128], P('dp', 'feat'), may hold values from 0 to 0.03125
- w_two: bfloat16 [2, 256, 256], replicated, may hold values from -0.375 to 0.375
- b_two: float32 [256], replicated, may hold values from -3 to 3
- cotangent: bfloat16 [2, 2048, 256], P('dp', 'feat'), may hold values from -0.09375 to 0.09375
Outputs:
- out_two: bfloat16 [2, 2048, 256], P('dp', 'feat')
- grad_w_one: float32 [2, 1024, 256], P(None, 'feat')
- grad_b_one: float32 [256], replicated
- grad_w_two: float32 [2, 256, 256], replicated
- grad_b_two: float32 [256], replicated
Inputs may be any that keep to these rules, and one draw needn't show every extreme that they name: `tile_counts`: the first 2048 source nodes are the minibatch's nodes themselves; in every replica some row block has all 4 slots live.
All inputs are finite; a program needn't handle non-finite values.
Results may differ from a plain program's by a relative error of at most 0.0085.
Values may be sent and summed in bfloat16 or wider, within the bound.
A program may use at most 64 MiB of HBM per device.

v0:
```python
import jax
import jax.numpy as jnp
from jax import lax
from jax.sharding import PartitionSpec as P


def local(
    x_feat, tiles_one, tile_cols, tile_counts, w_one, b_one, adj_two, w_two, b_two, cotangent
):
    x_slice = x_feat[0]
    slice_width = x_slice.shape[0]
    parts = lax.axis_size("feat")
    tile = adj_two.shape[-1]
    slot_cap = tiles_one.shape[1]
    node_total = tile * parts
    blocks = x_slice.reshape(slice_width, -1, tile)
    slot_live = (jnp.arange(slot_cap) < tile_counts[0, 0]).astype(jnp.bfloat16)
    own_tiles = tiles_one[0] * slot_live[:, None, None]
    contract_first = (((0,), (0,)), ((), ()))
    w_full = lax.all_gather(w_one, "feat", axis=1, tiled=True)
    tile_vals = lax.all_gather(own_tiles, "feat", axis=0, tiled=True)
    cols = lax.all_gather(tile_cols[0], "feat", axis=0, tiled=True)
    count = cols.shape[0]
    picked = jnp.take(blocks, cols, axis=1)
    contrib = jnp.einsum("fpt,put->pfu", picked, tile_vals, preferred_element_type=jnp.float32)
    row_block = jnp.arange(count) // slot_cap
    onehot = (row_block[:, None] == jnp.arange(parts)[None, :]).astype(jnp.float32)
    folded = jnp.einsum("pr,pfu->rfu", onehot, contrib)
    agg_one = folded.transpose(1, 0, 2).reshape(slice_width, node_total).astype(jnp.bfloat16)
    x_self = x_slice[:, :node_total]
    stacked = jnp.stack([x_self, agg_one])
    moved = lax.all_to_all(stacked, "feat", split_axis=2, concat_axis=1, tiled=True)
    z_one = jnp.einsum("kfn,kfh->nh", moved, w_full, preferred_element_type=jnp.float32) + b_one
    h_one = jax.nn.silu(z_one).astype(jnp.bfloat16)
    adjacency = adj_two[0]
    agg_two = jnp.dot(adjacency, h_one, preferred_element_type=jnp.float32).astype(jnp.bfloat16)
    z_two = jnp.dot(h_one, w_two[0], preferred_element_type=jnp.float32)
    z_two = z_two + jnp.dot(agg_two, w_two[1], preferred_element_type=jnp.float32) + b_two
    out_two = z_two.astype(jnp.bfloat16)[None]
    grad_out = cotangent[0]
    contract_last = (((1,), (1,)), ((), ()))
    dagg_two = lax.dot_general(
        grad_out, w_two[1], contract_last, preferred_element_type=jnp.float32
    ).astype(jnp.bfloat16)
    dh_one = lax.dot_general(grad_out, w_two[0], contract_last, preferred_element_type=jnp.float32)
    dh_one = dh_one + lax.dot_general(
        adjacency, dagg_two, contract_first, preferred_element_type=jnp.float32
    )
    sig = jax.nn.sigmoid(z_one)
    dz_one = (dh_one * sig * (1.0 + z_one * (1.0 - sig))).astype(jnp.bfloat16)
    local_w2 = jnp.stack(
        [
            lax.dot_general(h_one, grad_out, contract_first, preferred_element_type=jnp.float32),
            lax.dot_general(agg_two, grad_out, contract_first, preferred_element_type=jnp.float32),
        ]
    )
    local_b2 = jnp.sum(grad_out.astype(jnp.float32), axis=0)
    local_b1 = jnp.sum(dz_one.astype(jnp.float32), axis=0)
    grad_w2, grad_b2, grad_b1 = lax.psum((local_w2, local_b2, local_b1), ("feat", "dp"))
    piece = lax.all_gather(dz_one, "feat", axis=0, tiled=True)
    first = jnp.dot(x_self, piece, preferred_element_type=jnp.float32)
    second = jnp.dot(agg_one, piece, preferred_element_type=jnp.float32)
    local_w1 = jnp.stack([first, second])
    grad_w1 = lax.psum(local_w1, "dp")
    return (out_two, grad_w1, grad_b1, grad_w2, grad_b2)


def solution(mesh):
    in_specs = (
        P("dp", "feat", None),
        P("dp", "feat", None, None),
        P("dp", "feat"),
        P("dp", "feat"),
        P(None, "feat", None),
        P(),
        P("dp", "feat", None),
        P(),
        P(),
        P("dp", "feat", None),
    )
    out_specs = (P("dp", "feat", None), P(None, "feat", None), P(), P(), P())
    return jax.shard_map(local, mesh=mesh, in_specs=in_specs, out_specs=out_specs, check_vma=False)
```

profile of v0, /device:TPU:0, one launch (start us, length us, event | category | flops | bytes accessed | tf_op | source)
XLA Modules:
  0.0 302.3 jit_solution(3218296160944779400)
XLA Ops:
  7.9 1.6 bitcast_multiply_fusion
  10.3 1.2 dynamic-slice
  13.0 13.7 %all-reduce = s32[64]{0:T(128)S(1)} all-reduce(s32[64]{0:T(128)S(1)} %bitcast_dynamic-update-slice_fusion), channel_id=2, replica_groups=mesh['feat'=16,'dp'=2] {'feat'}, use_global_device_ids=true, to_apply=%add | all-reduce | flops 64 | bytes 512 | tf_op jit(solution)/shard_map/all_gather | solution.py:22
  26.7 1.7 slice_bitcast_fusion
  28.4 2.5 copy.37
  30.9 0.9 copy.28
  31.8 1.7 gather_fusion
  33.4 21.4 %all-gather.5.cloned.1.call-done = bf16[64,128,128]{2,1,0:T(8,128)(2,1)} async-done(((bf16[4,128,128]{2,1,0:T(8,128)(2,1)}), bf16[64,128,128]{2,1,0:T(8,128)(2,1)}) %all-gather.5.cloned.1.call-update) | async-done | bytes 2097168 | tf_op jit(solution)/shard_map/all_gather | solution.py:21
  54.8 3.5 %fusion.12 = bf16[64,64,128]{2,1,0:T(8,128)(2,1)S(1)} fusion(bf16[64,128,128]{2,1,0:T(8,128)(2,1)} %all-gather.5.cloned.1.call-done, bf16[64,64,128]{2,1,0:T(8,128)(2,1)} %gather_fusion, pred[64]{0:T(512)(128)(4,1)S(1)} %compare_and_fusion), kind=kOutput, calls=%fused_computation.21 | convolution fusion | flops 134742016 | bytes 4194368 | tf_op jit(solution)/shard_map/fpt,put->pfu/dot_general | solution.py:25
  60.0 1.5 reshape.66
  61.5 3.6 %all-to-all-start = ((bf16[16,2,8192]{2,1,0:T(2,128)(2,1)}), bf16[16,2,8192]{2,1,0:T(2,128)(2,1)S(1)}, u32[]{:S(2)}, u32[]{:S(2)}) async-start(bf16[16,2,8192]{2,1,0:T(2,128)(2,1)} %reshape.66), calls=%async_computation | async-start | bytes 1048576 | tf_op jit(solution)/shard_map/all_to_all | solution.py:32
  65.5 15.3 %all-to-all-done = bf16[16,2,8192]{2,1,0:T(2,128)(2,1)S(1)} async-done(((bf16[16,2,8192]{2,1,0:T(2,128)(2,1)}), bf16[16,2,8192]{2,1,0:T(2,128)(2,1)S(1)}, u32[]{:S(2)}, u32[]{:S(2)}) %all-to-all-start) | async-done | bytes 524320 | tf_op jit(solution)/shard_map/all_to_all | solution.py:32
  82.2 14.5 %all-gather.7.cloned.1.call-done = bf16[2,1024,256]{2,1,0:T(8,128)(2,1)} async-done(((bf16[2,64,256]{2,1,0:T(8,128)(2,1)}), bf16[2,1024,256]{2,1,0:T(8,128)(2,1)}) %all-gather.7.cloned.1.call-update) | async-done | bytes 1048592 | tf_op jit(solution)/shard_map/all_gather | solution.py:20
  96.7 1.6 multiply_convert_fusion
  98.3 0.8 convert_reduce_fusion.1
  100.8 35.6 %all-gather.9.cloned.1.call-done = bf16[2048,256]{1,0:T(8,128)(2,1)} async-done(((bf16[128,256]{1,0:T(8,128)(2,1)}), bf16[2048,256]{1,0:T(8,128)(2,1)}) %all-gather.9.cloned.1.call-update) | async-done | bytes 1048592 | tf_op jit(solution)/shard_map/all_gather | solution.py:60
  136.4 1.6 convolution_bitcast_fusion.4
  138.0 1.5 convolution_bitcast_fusion.5
  140.3 39.0 %all-reduce.1 = (f32[256]{0:T(256)}, f32[256]{0:T(256)}) all-reduce(f32[256]{0:T(256)S(1)} %get-tuple-element.9, f32[256]{0:T(256)S(1)} %convert_reduce_fusion), channel_id=1, replica_groups=mesh['feat'=16,'dp'=2] {'feat','dp'}, use_global_device_ids=true, to_apply=%region_2.3 | all-reduce | flops 512 | bytes 4096 | tf_op jit(solution)/shard_map/psum | solution.py:59
  179.4 0.8 fusion.11
  180.2 88.9 %all-reduce.7.cloned.1.call-done = f32[2,256,256]{2,1,0:T(8,128)} async-done(((f32[2,256,256]{2,1,0:T(8,128)}), f32[2,256,256]{2,1,0:T(8,128)}) %all-reduce.7.cloned.1.call-update) | async-done | bytes 524304 | tf_op jit(solution)/shard_map/psum | solution.py:59
  269.1 23.2 %all-reduce.5.cloned.1.call-done = f32[2,64,256]{2,1,0:T(8,128)} async-done(((f32[2,64,256]{2,1,0:T(8,128)}), f32[2,64,256]{2,1,0:T(8,128)}) %all-reduce.5.cloned.1.call-update) | async-done | bytes 131088 | tf_op jit(solution)/shard_map/psum | solution.py:64
  292.4 1.6 copy.51
  294.0 1.9 copy.52
  (43 shorter events, 7.4 us)
Async XLA Ops:
  7.2 57.9 %copy-start = (bf16[1,128,128]{2,1,0:T(8,128)(2,1)S(1)}, bf16[1,128,128]{2,1,0:T(8,128)(2,1)}, u32[]{:S(2)}) copy-start(bf16[1,128,128]{2,1,0:T(8,128)(2,1)} %param.16) | copy-start | bytes 98308
  7.2 47.6 %all-gather.5.cloned.1.call-start = ((), (), s32[]{:S(2)}) async-start(), calls=%async_computation.1 | async-start | bytes 2228224 | tf_op jit(solution)/shard_map/all_gather | solution.py:21
  9.5 87.2 %all-gather.7.cloned.1.call-start = ((), (), s32[]{:S(2)}) async-start(), calls=%async_computation.2 | async-start | bytes 1114112 | tf_op jit(solution)/shard_map/all_gather | solution.py:20
  33.4 25.7 %copy-start.1 = (bf16[1,64,2048]{2,1,0:T(8,128)(2,1)S(1)}, bf16[1,64,2048]{2,1,0:T(8,128)(2,1)}, u32[]{:S(2)}) copy-start(bf16[1,64,2048]{2,1,0:T(8,128)(2,1)} %slice_bitcast_fusion) | copy-start | bytes 786436
  58.3 6.8 %copy-start.2 = (bf16[1,128,256]{2,1,0:T(8,128)(2,1)S(1)}, bf16[1,128,256]{2,1,0:T(8,128)(2,1)}, u32[]{:S(2)}) copy-start(bf16[1,128,256]{2,1,0:T(8,128)(2,1)} %param.19) | copy-start | bytes 196612
  58.3 6.8 %copy-start.3 = (bf16[2,256,256]{2,1,0:T(8,128)(2,1)S(1)}, bf16[2,256,256]{2,1,0:T(8,128)(2,1)}, u32[]{:S(2)}) copy-start(bf16[2,256,256]{2,1,0:T(8,128)(2,1)} %param.17) | copy-start | bytes 786436
  59.9 36.8 %copy-start.4 = (f32[256]{0:T(256)S(1)}, f32[256]{0:T(256)}, u32[]{:S(2)}) copy-start(f32[256]{0:T(256)} %param.15) | copy-start | bytes 3076
  61.5 19.3 %all-to-all-start = ((bf16[16,2,8192]{2,1,0:T(2,128)(2,1)}), bf16[16,2,8192]{2,1,0:T(2,128)(2,1)S(1)}, u32[]{:S(2)}, u32[]{:S(2)}) async-start(bf16[16,2,8192]{2,1,0:T(2,128)(2,1)} %reshape.66), calls=%async_computation | async-start | bytes 1048576 | tf_op jit(solution)/shard_map/all_to_all | solution.py:32
  65.0 71.3 %all-gather.9.cloned.1.call-start = ((), (), s32[]{:S(2)}) async-start(), calls=%async_computation.3 | async-start | bytes 1114112 | tf_op jit(solution)/shard_map/all_gather | solution.py:60
  98.3 81.1 %copy-start.5 = (f32[256]{0:T(256)S(1)}, f32[256]{0:T(256)}, u32[]{:S(2)}) copy-start(f32[256]{0:T(256)} %param.18) | copy-start | bytes 3076
  99.2 169.9 %all-reduce.7.cloned.1.call-start = ((), (), s32[]{:S(2)}) async-start(), calls=%async_computation.5 | async-start | bytes 1048576 | tf_op jit(solution)/shard_map/psum | solution.py:59
  100.7 191.7 %all-reduce.5.cloned.1.call-start = ((), (), s32[]{:S(2)}) async-start(), calls=%async_computation.4 | async-start | bytes 262144 | tf_op jit(solution)/shard_map/psum | solution.py:64
Sparse Core Ops, SparseCore 0:
  10.7 44.0 all-gather.4
  57.0 39.6 all-gather.6
  99.5 36.8 all-gather.8
  142.1 127.0 all-reduce.6
  271.9 20.4 all-reduce.4
where the time goes:
time: 303 us; the launch traced here: 302 us
  waiting for transfers between devices  200 us (66%)
  blocking collectives  52.8 us (17%)
  local copies, waits for them, and re-layouts  16 us (5%)
  between operations  15.3 us (5%)
  matrix products  11.6 us (4%)
  starting transfers between devices  3.78 us (1%)
  other arithmetic  3.25 us (1%)
    psum x1, waiting for transfers between devices, local(): lax.psum((local_w2, local_b2, local_b1), ('feat', 'dp'))  88.9 us
    psum x1, blocking collectives, local(): lax.psum((local_w2, local_b2, local_b1), ('feat', 'dp'))  39 us
    all_gather x1, waiting for transfers between devices, local(): piece = lax.all_gather(dz_one, 'feat', axis=0, tiled=True)  35.6 us
    psum x1, waiting for transfers between devices, local(): grad_w1 = lax.psum(local_w1, 'dp')  23.2 us
    all_gather x1, waiting for transfers between devices, local(): tile_vals = lax.all_gather(own_tiles, 'feat', axis=0, tiled=True)  21.4 us
    all_to_all x1, waiting for transfers between devices, local(): lax.all_to_all(stacked, 'feat', split_axis=2, concat_axis=1, tiled=True)  15.3 us
    all_gather x1, waiting for transfers between devices, local(): w_full = lax.all_gather(w_one, 'feat', axis=1, tiled=True)  14.5 us
    all_gather x1, blocking collectives, local(): cols = lax.all_gather(tile_cols[0], 'feat', axis=0, tiled=True)  13.7 us
  transfers between devices with their start and end apart: 6, of which 6 were waited for; matrix products, arithmetic and copies ran while one was open for 8% of the time, Pallas kernels for 0%

commit v1 on v0

v1 whole, which is shorter than its diff:
```python
import functools
import math

import jax
import jax.numpy as jnp
from jax import lax
from jax.experimental import pallas as pl
from jax.experimental.pallas import tpu as pltpu
from jax.sharding import PartitionSpec as P

BF = jnp.bfloat16
F32 = jnp.float32


def dot(a, b, dims=((1,), (0,))):
    return lax.dot_general(a, b, (dims, ((), ())), preferred_element_type=F32)


def grid_of(n):
    x = max(math.isqrt(n // 4), 1)
    while (n // 2) % x:
        x -= 1
    return n // 2 // x, x


def kernel(
    n, dp, zs, xs,
    x_hbm, tiles, cols, counts, w1, b1, adj, w2, b2, cot,
    out2, gw1, gb1, gw2, gb2,
    xv, pack, mv, agg, dzb, colv, coli, cols_s, dh_s, acc,
    w2s, w2r, g2s, g2r, bs, bb, dps, dpr, w1s, w1r,
    ag_send, ag_recv, dz_send, dz_recv, pair_sem, loc_sem,
):
    me = lax.axis_index("feat")
    my_dp = lax.axis_index("dp")
    core = lax.rem(me, 2)
    chip = lax.div(me, 2)
    xx = lax.rem(chip, xs)
    zz = lax.div(chip, xs)
    sl = w1.shape[1]
    tile = adj.shape[0]
    slots = tiles.shape[0]
    trows = slots * tile
    hid = w1.shape[2]
    half_w = hid // 2
    rows = w2s.shape[1]

    def index(z, x, c):
        return (z * xs + x) * 2 + c

    def remote(src, dst, ssem, rsem, peer, axis="feat"):
        return pltpu.make_async_remote_copy(
            src_ref=src, dst_ref=dst, send_sem=ssem, recv_sem=rsem,
            device_id={axis: peer}, device_id_type=pl.DeviceIdType.MESH,
        )

    def wait_for(ref, sem):
        pltpu.make_async_copy(ref, ref, sem).wait()

    @pl.loop(0, xv.shape[0])
    def _(b):
        at = pl.multiple_of(b * tile, tile)
        pltpu.make_async_copy(x_hbm.at[:, pl.ds(at, tile)], xv.at[b], loc_sem.at[0]).start()

    barrier = pltpu.get_barrier_semaphore()

    @pl.loop(1, n)
    def _(k):
        pl.semaphore_signal(
            barrier, inc=1, device_id={"feat": lax.rem(me + k, n)}, device_id_type=pl.DeviceIdType.MESH
        )

    @pl.loop(1, dp)
    def _(k):
        pl.semaphore_signal(
            barrier, inc=1, device_id={"dp": lax.rem(my_dp + k, dp)}, device_id_type=pl.DeviceIdType.MESH
        )

    count = counts[0, 0]
    lane = lax.broadcasted_iota(jnp.int32, (1, 128), 1)
    info = jnp.zeros((1, 128), jnp.int32)
    for s in range(slots):
        live = jnp.minimum(jnp.maximum(count - s, 0), 1).astype(F32)
        pack[me, s * tile : (s + 1) * tile, :] = (tiles[s].astype(F32) * live).astype(BF)
        info = jnp.where(lane == s, cols[0, s], info)
    colv[...] = info
    for k in range(2):
        for h in range(2):
            at = trows + (k * 2 + h) * sl
            pack[me, at : at + sl, :] = w1[k, :, h * half_w : (h + 1) * half_w]
    bs[...] = jnp.zeros_like(bs)
    bs[1:2, :] = jnp.sum(cot[...].astype(F32), axis=0, keepdims=True)
    pl.semaphore_wait(barrier, n - 1 + dp - 1)

    class Gather:
        def __init__(self, buf, send, recv):
            self.buf, self.send, self.recv = buf, send, recv
            self.half = buf.shape[1] // 2

        def view(self, h, src):
            return self.buf.at[src, pl.ds(h * self.half, self.half), :]

        def copy(self, h, src, slot, peer):
            v = self.view(h, src)
            return remote(v, v, self.send.at[h, src, slot], self.recv.at[h, src], peer)

        def wait(self, h, src):
            wait_for(self.view(h, src), self.recv.at[h, src])

        def up(self, h, src, act):
            @pl.when(zz < zs - 1)
            def _():
                act(self.copy(h, src, 0, index(zz + 1, xx, core)))

        def down(self, h, src, act):
            @pl.when(zz > 0)
            def _():
                act(self.copy(h, src, 1, index(zz - 1, xx, core)))

        def across(self, h, src, act):
            for k in range(1, xs):
                act(self.copy(h, src, 1 + k, index(zz, lax.rem(xx + k, xs), core)))

        def sibling(self, h, src, act):
            act(self.copy(h, src, xs + 1, index(zz, xx, 1 - core)))

        def walk(self, act, first, arrive):
            for h in (1, 0):
                self.across(h, me, act)
                self.up(h, me, act)
                self.down(h, me, act)
                self.sibling(h, me, act)
            first()
            for k in range(1, xs):
                src = index(zz, lax.rem(xx + k, xs), core)
                arrive(1, src)
                self.up(1, src, act)
                self.down(1, src, act)
                self.sibling(1, src, act)

            @pl.loop(1, zs)
            def _(k):
                @pl.when(zz - k >= 0)
                def _():
                    src = index(zz - k, xx, core)
                    arrive(0, src)
                    self.up(0, src, act)
                    self.across(0, src, act)
                    self.sibling(0, src, act)

                @pl.when(zz + k < zs)
                def _():
                    src = index(zz + k, xx, core)
                    arrive(0, src)
                    self.down(0, src, act)
                    self.across(0, src, act)
                    self.sibling(0, src, act)

                for j in range(xs):
                    other = lax.rem(xx + j, xs)

                    @pl.when(zz - k >= 0)
                    def _():
                        src = index(zz - k, other, core)
                        arrive(1, src)
                        self.up(1, src, act)
                        self.sibling(1, src, act)

                    @pl.when(zz + k < zs)
                    def _():
                        src = index(zz + k, other, core)
                        arrive(1, src)
                        self.down(1, src, act)
                        self.sibling(1, src, act)

            @pl.loop(0, zs)
            def _(k):
                z = lax.rem(zz + k, zs)
                for j in range(1, xs):
                    src = index(z, lax.rem(xx + j, xs), core)
                    arrive(0, src)
                    self.sibling(0, src, act)

        def run(self, first):
            self.walk(lambda c: c.start(), first, self.wait)

        def finish(self):
            self.walk(lambda c: c.wait_send(), lambda: None, lambda h, s: None)

    def backward_start():
        dagg = dot(cot[...], w2[1], ((1,), (1,))).astype(BF)
        dh = dot(cot[...], w2[0], ((1,), (1,)))
        dh_s[...] = dh + dot(adj[...], dagg, ((0,), (0,)))

    def features_out():
        wait_for(xv, loc_sem.at[0])

        @pl.loop(1, n)
        def _(k):
            p = lax.rem(me + k, n)
            remote(
                xv.at[p], mv.at[0, me], pair_sem.at[2], pair_sem.at[3], p,
            ).start()

        pltpu.make_async_copy(
            xv.at[me], mv.at[0, me], pair_sem.at[3]
        ).start()

    @pl.loop(1, n)
    def _(k):
        remote(colv, coli.at[me], pair_sem.at[0], pair_sem.at[1], lax.rem(me + k, n)).start()

    pltpu.make_async_copy(colv, coli.at[me], pair_sem.at[1]).start()

    def before_relay():
        features_out()
        backward_start()

    gather = Gather(pack, ag_send, ag_recv)
    gather.run(before_relay)
    wait_for(coli, pair_sem.at[1])
    to_smem = pltpu.make_async_copy(coli, cols_s, loc_sem.at[1])
    to_smem.start()
    to_smem.wait()

    def aggregate(r):
        total = jnp.zeros((sl, tile), F32)
        for s in range(slots):
            total += dot(xv[cols_s[r, 0, s]], pack[r, s * tile : (s + 1) * tile, :], ((1,), (1,)))
        agg[r] = total.astype(BF)

        @pl.when(r != me)
        def _():
            remote(agg.at[r], mv.at[1, me], pair_sem.at[4], pair_sem.at[5], r).start()

        @pl.when(r == me)
        def _():
            pltpu.make_async_copy(agg.at[r], mv.at[1, me], pair_sem.at[5]).start()

    half_n = n // 2

    @pl.loop(0, half_n)
    def _(j):
        aggregate(lax.rem(chip + j, half_n) * 2 + core)

    @pl.loop(0, half_n)
    def _(j):
        r = lax.rem(chip + j, half_n) * 2 + 1 - core
        gather.wait(0, r)
        gather.wait(1, r)
        aggregate(r)

    def project(k):
        at = trows + k * 2 * sl
        w = jnp.concatenate(
            [
                pack[:, at + h * sl : at + (h + 1) * sl, :].reshape(n * sl, half_w)
                for h in range(2)
            ],
            axis=1,
        )
        return dot(mv[k].reshape(n * sl, tile), w, ((0,), (0,)))

    wait_for(mv.at[0], pair_sem.at[3])
    acc[...] = project(0) + b1[...]
    wait_for(mv.at[1], pair_sem.at[5])
    z = acc[...] + project(1)
    sig = 1.0 / (1.0 + jnp.exp(-z))
    h_one = (z * sig).astype(BF)
    dz = (dh_s[...] * sig * (1.0 + z * (1.0 - sig))).astype(BF)
    dzb[me] = dz
    bs[0:1, :] = jnp.sum(dz.astype(F32), axis=0, keepdims=True)

    def forward():
        agg_two = dot(adj[...], h_one).astype(BF)
        g0 = dot(h_one, cot[...], ((0,), (0,)))
        g1 = dot(agg_two, cot[...], ((0,), (0,)))
        w2s[: n // 2] = g0.reshape(n // 2, rows, hid).astype(w2s.dtype)
        w2s[n // 2 :] = g1.reshape(n // 2, rows, hid).astype(w2s.dtype)

        @pl.loop(1, n)
        def _(k):
            p = lax.rem(me + k, n)
            remote(w2s.at[p], w2r.at[me], pair_sem.at[6], pair_sem.at[7], p).start()
            remote(bs, bb.at[me], pair_sem.at[8], pair_sem.at[9], p).start()

        pltpu.make_async_copy(w2s.at[me], w2r.at[me], pair_sem.at[7]).start()
        pltpu.make_async_copy(bs, bb.at[me], pair_sem.at[9]).start()
        z2 = dot(h_one, w2[0]) + dot(agg_two, w2[1]) + b2[...]
        out2[...] = z2.astype(BF)

    dgather = Gather(dzb, dz_send, dz_recv)
    dgather.run(forward)

    wait_for(w2r, pair_sem.at[7])
    wait_for(bb, pair_sem.at[9])
    dps[0:rows, :] = jnp.sum(w2r[...].astype(F32), axis=0)
    dps[rows:, :] = jnp.sum(bb[...], axis=0)

    def over_replicas(src, dst, ssem, rsem):
        @pl.loop(1, dp)
        def _(k):
            remote(src, dst.at[my_dp], ssem, rsem, lax.rem(my_dp + k, dp), "dp").start()

        pltpu.make_async_copy(src, dst.at[my_dp], rsem).start()

    over_replicas(dps, dpr, pair_sem.at[10], pair_sem.at[11])

    acc[...] = jnp.zeros_like(acc)

    def weight(r):
        lhs = jnp.concatenate([xv[r], agg[r]], axis=0)
        acc[0 : 2 * sl, :] += dot(lhs, dzb[r])

    @pl.loop(0, half_n)
    def _(j):
        weight(lax.rem(chip + j, half_n) * 2 + core)

    wait_for(dpr, pair_sem.at[11])
    total = dpr[0]
    for k in range(1, dp):
        total = total + dpr[k]
    g2s[...] = total[0:rows].astype(g2s.dtype)
    gb1[...] = total[rows : rows + 1]
    gb2[...] = total[rows + 1 : rows + 2]

    @pl.loop(1, n)
    def _(k):
        remote(g2s, g2r.at[me], pair_sem.at[12], pair_sem.at[13], lax.rem(me + k, n)).start()

    pltpu.make_async_copy(g2s, g2r.at[me], pair_sem.at[13]).start()

    @pl.loop(0, half_n)
    def _(j):
        r = lax.rem(chip + j, half_n) * 2 + 1 - core
        dgather.wait(0, r)
        dgather.wait(1, r)
        weight(r)

    w1s[...] = acc[0 : 2 * sl, :].astype(w1s.dtype)
    over_replicas(w1s, w1r, pair_sem.at[14], pair_sem.at[15])
    gather.finish()
    dgather.finish()

    def sent(ref, sem):
        wait_for(ref, sem)

    sent(coli.at[pl.ds(0, n - 1)], pair_sem.at[0])
    sent(mv.at[0, pl.ds(0, n - 1)], pair_sem.at[2])
    sent(mv.at[1, pl.ds(0, n - 1)], pair_sem.at[4])
    sent(w2r.at[pl.ds(0, n - 1)], pair_sem.at[6])
    sent(bb.at[pl.ds(0, n - 1)], pair_sem.at[8])
    wait_for(g2r, pair_sem.at[13])
    gw2[...] = g2r[...].astype(F32).reshape(n * rows, hid)
    sent(g2r.at[pl.ds(0, n - 1)], pair_sem.at[12])
    if dp > 1:
        sent(dpr.at[pl.ds(0, dp - 1)], pair_sem.at[10])
    wait_for(w1r, pair_sem.at[15])
    total = w1r[0].astype(F32)
    for k in range(1, dp):
        total = total + w1r[k].astype(F32)
    gw1[...] = total
    if dp > 1:
        sent(w1r.at[pl.ds(0, dp - 1)], pair_sem.at[14])


def local(n, dp, x_feat, tiles_one, tile_cols, tile_counts, w_one, b_one, adj_two, w_two, b_two, cotangent):
    zs, xs = grid_of(n)
    sl, width = x_feat.shape[1:]
    tile = adj_two.shape[-1]
    slots = tiles_one.shape[1]
    hid = w_one.shape[2]
    rows = 2 * hid // n
    narrow = BF if rows % 16 == 0 else F32
    packed = slots * tile + 4 * sl
    vmem = pl.BlockSpec(memory_space=pltpu.VMEM)
    smem = pl.BlockSpec(memory_space=pltpu.SMEM)
    dma = pltpu.SemaphoreType.DMA
    out2, gw1, gb1, gw2, gb2 = pl.pallas_call(
        functools.partial(kernel, n, dp, zs, xs),
        out_shape=(
            jax.ShapeDtypeStruct((tile, hid), BF),
            jax.ShapeDtypeStruct((2 * sl, hid), F32),
            jax.ShapeDtypeStruct((1, hid), F32),
            jax.ShapeDtypeStruct((2 * hid, hid), F32),
            jax.ShapeDtypeStruct((1, hid), F32),
        ),
        in_specs=[
            pl.BlockSpec(memory_space=pl.ANY), vmem, smem, smem, vmem, vmem, vmem, vmem, vmem, vmem,
        ],
        out_specs=(vmem,) * 5,
        scratch_shapes=[
            pltpu.VMEM((width // tile, sl, tile), BF),
            pltpu.VMEM((n, packed, tile), BF),
            pltpu.VMEM((2, n, sl, tile), BF),
            pltpu.VMEM((n, sl, tile), BF),
            pltpu.VMEM((n, tile, hid), BF),
            pltpu.VMEM((1, 128), jnp.int32),
            pltpu.VMEM((n, 1, 128), jnp.int32),
            pltpu.SMEM((n, 1, 128), jnp.int32),
            pltpu.VMEM((tile, hid), F32),
            pltpu.VMEM((max(tile, 2 * sl), hid), F32),
            pltpu.VMEM((n, rows, hid), narrow),
            pltpu.VMEM((n, rows, hid), narrow),
            pltpu.VMEM((rows, hid), narrow),
            pltpu.VMEM((n, rows, hid), narrow),
            pltpu.VMEM((8, hid), F32),
            pltpu.VMEM((n, 8, hid), F32),
            pltpu.VMEM((rows + 8, hid), F32),
            pltpu.VMEM((dp, rows + 8, hid), F32),
            pltpu.VMEM((2 * sl, hid), BF),
            pltpu.VMEM((dp, 2 * sl, hid), BF),
            dma((2, n, xs + 2)),
            dma((2, n)),
            dma((2, n, xs + 2)),
            dma((2, n)),
            dma((16,)),
            dma((2,)),
        ],
        compiler_params=pltpu.CompilerParams(
            collective_id=0, has_side_effects=True, vmem_limit_bytes=48 * 1024 * 1024
        ),
    )(
        x_feat[0], tiles_one[0], tile_cols, tile_counts, w_one, b_one[None], adj_two[0], w_two,
        b_two[None], cotangent[0],
    )
    return (
        out2[None], gw1.reshape(2, sl, hid), gb1[0], gw2.reshape(2, hid, hid), gb2[0],
    )


def solution(mesh):
    in_specs = (
        P("dp", "feat", None),
        P("dp", "feat", None, None),
        P("dp", "feat"),
        P("dp", "feat"),
        P(None, "feat", None),
        P(),
        P("dp", "feat", None),
        P(),
        P(),
        P("dp", "feat", None),
    )
    out_specs = (P("dp", "feat", None), P(None, "feat", None), P(), P(), P())
    return jax.shard_map(
        functools.partial(local, mesh.shape["feat"], mesh.shape["dp"]),
        mesh=mesh, in_specs=in_specs, out_specs=out_specs, check_vma=False,
    )
```

time: 303 us -> 86.2 us (0.28)
  waiting for transfers between devices: 200 us -> 0 us
  Pallas kernels: 0 us -> 73 us
  blocking collectives: 52.8 us -> 0 us
  between operations: 15.3 us -> 1.31 us
  matrix products: 11.6 us -> 0 us
  local copies, waits for them, and re-layouts: 16 us -> 11.5 us
  starting transfers between devices: 3.78 us -> 0 us
  other arithmetic: 3.25 us -> 0 us
    psum x2 -> x0, waiting for transfers between devices: 112 us -> none  [the longest x1 88.9 us: local(): lax.psum((local_w2, local_b2, local_b1), ('feat', 'dp'))]
    pallas_call x0 -> x1, Pallas kernels: none -> 73 us  [local(): pl.pallas_call(functools.partial(kernel, n, dp, zs, xs), out_shape=(jax.S...]
    all_gather x3 -> x0, waiting for transfers between devices: 71.5 us -> none  [the longest x1 35.6 us: local(): piece = lax.all_gather(dz_one, 'feat', axis=0, tiled=True)]
    psum x1 -> x0, blocking collectives: 39 us -> none  [local(): lax.psum((local_w2, local_b2, local_b1), ('feat', 'dp'))]
    all_to_all x1 -> x0, waiting for transfers between devices: 15.3 us -> none  [local(): lax.all_to_all(stacked, 'feat', split_axis=2, concat_axis=1, tiled=True)]
    all_gather x1 -> x0, blocking collectives: 13.7 us -> none  [local(): cols = lax.all_gather(tile_cols[0], 'feat', axis=0, tiled=True)]
    dot_general x12 -> x0, matrix products: 11.6 us -> none  [the longest x1 3.45 us: local(): jnp.einsum('fpt,put->pfu', picked, tile_vals, preferred_element_type=jnp....]
    all_to_all x1 -> x0, starting transfers between devices: 3.57 us -> none  [local(): lax.all_to_all(stacked, 'feat', split_axis=2, concat_axis=1, tiled=True)]
  transfers between devices with their start and end apart: 6 -> 0, of which waited for: 6 -> 0; matrix products, arithmetic and copies ran while one was open for 8% -> 0% of each run, Pallas kernels for 0% -> 0%
where the time goes in v1:
time: 86.2 us; the launch traced here: 85.8 us
  Pallas kernels  73 us (85%)
  local copies, waits for them, and re-layouts  11.5 us (13%)
  between operations  1.31 us (2%)
    pallas_call x1, Pallas kernels, local(): pl.pallas_call(functools.partial(kernel, n, dp, zs, xs), out_shape=(jax.S...  73 us
    unnamed x23, local copies, waits for them, and re-layouts  11.5 us

profile of v1, /device:TPU:0, one launch (start us, length us, event | category | flops | bytes accessed | tf_op | source)
XLA Modules:
  0.0 85.8 jit_solution(8377218759692541104)
XLA Ops:
  1.3 0.0 copy-start
  1.3 2.0 %copy-done = bf16[1,64,26624]{2,1,0:T(8,128)(2,1)S(1)} copy-done((bf16[1,64,26624]{2,1,0:T(8,128)(2,1)S(1)}, bf16[1,64,26624]{2,1,0:T(8,128)(2,1)}, u32[]{:S(2)}) %copy-start) | copy-done | bytes 3407896
  3.2 0.0 copy-start.1
  3.2 0.9 %copy-done.1 = bf16[2,256,256]{2,1,0:T(8,128)(2,1)S(1)} copy-done((bf16[2,256,256]{2,1,0:T(8,128)(2,1)S(1)}, bf16[2,256,256]{2,1,0:T(8,128)(2,1)}, u32[]{:S(2)}) %copy-start.1) | copy-done | bytes 262168
  4.2 0.0 copy-start.2
  4.2 0.9 %copy-done.2 = bf16[1,4,128,128]{3,2,1,0:T(8,128)(2,1)S(1)} copy-done((bf16[1,4,128,128]{3,2,1,0:T(8,128)(2,1)S(1)}, bf16[1,4,128,128]{3,2,1,0:T(8,128)(2,1)}, u32[]{:S(2)}) %copy-start.2) | copy-done | bytes 131096
  5.1 0.0 copy-start.3
  5.1 0.8 copy-done.3
  5.9 0.0 copy-start.4
  5.9 0.8 copy-done.4
  6.8 0.0 copy-start.5
  6.8 0.8 copy-done.5
  7.5 0.0 copy-start.6
  7.5 0.7 copy-done.6
  8.2 0.0 copy-start.7
  8.2 0.7 copy-done.7
  8.9 0.0 copy-start.8
  8.9 0.7 copy-done.8
  9.6 73.0 %shard_map.137 = (bf16[128,256]{1,0:T(8,128)(2,1)S(1)}, f32[128,256]{1,0:T(8,128)S(1)}, f32[1,256]{1,0:T(1,128)S(1)}, f32[512,256]{1,0:T(8,128)S(1)}, f32[1,256]{1,0:T(1,128)S(1)}) custom-call(bf16[64,26624]{1,0:T(8,128)(2,1)S(1)} %bitcast.11, bf16[4,128,128]{2,1,0:T(8,128)(2,1)S(1)} %bitcast.13, s32[1,4]{1,0:T(1,128)S(1)} %copy-done.8, ...), custom_call_target="tpu_custom_call" | custom-call | tf_op jit(solution)/shard_map/pallas_call | solution.py:379
  82.6 0.6 copy.21
  83.2 0.7 copy.22
  83.9 0.6 copy.23
  84.4 0.8 copy.24
  85.2 0.6 copy.25
Async XLA Ops:
  1.3 2.0 %copy-start = (bf16[1,64,26624]{2,1,0:T(8,128)(2,1)S(1)}, bf16[1,64,26624]{2,1,0:T(8,128)(2,1)}, u32[]{:S(2)}) copy-start(bf16[1,64,26624]{2,1,0:T(8,128)(2,1)} %param.10) | copy-start | bytes 10223620
  3.2 0.9 %copy-start.1 = (bf16[2,256,256]{2,1,0:T(8,128)(2,1)S(1)}, bf16[2,256,256]{2,1,0:T(8,128)(2,1)}, u32[]{:S(2)}) copy-start(bf16[2,256,256]{2,1,0:T(8,128)(2,1)} %w2.1) | copy-start | bytes 786436
  4.2 0.9 %copy-start.2 = (bf16[1,4,128,128]{3,2,1,0:T(8,128)(2,1)S(1)}, bf16[1,4,128,128]{3,2,1,0:T(8,128)(2,1)}, u32[]{:S(2)}) copy-start(bf16[1,4,128,128]{3,2,1,0:T(8,128)(2,1)} %param.11) | copy-start | bytes 393220
  5.1 0.8 copy-start.3
  5.9 0.8 copy-start.4
  6.8 0.8 copy-start.5
  7.5 0.7 copy-start.6
  8.2 0.7 copy-start.7
  8.9 0.7 copy-start.8

commit v2 on v1

--- a/solution.py
+++ b/solution.py
@@ -25,10 +25,11 @@
 
 def kernel(
     n, dp, zs, xs,
-    x_hbm, tiles, cols, counts, w1, b1, adj, w2, b2, cot,
+    x_hbm, tiles_h, cols_h, counts_h, w1_h, b1_h, adj_h, w2_h, b2_h, cot_h,
     out2, gw1, gb1, gw2, gb2,
     xv, pack, mv, agg, dzb, colv, coli, cols_s, dh_s, acc,
     w2s, w2r, g2s, g2r, bs, bb, dps, dpr, w1s, w1r,
+    tiles, cols, counts, w1, b1, adj, w2, b2, cot,
     ag_send, ag_recv, dz_send, dz_recv, pair_sem, loc_sem,
 ):
     me = lax.axis_index("feat")
@@ -57,11 +58,17 @@
     def wait_for(ref, sem):
         pltpu.make_async_copy(ref, ref, sem).wait()
 
-    @pl.loop(0, xv.shape[0])
-    def _(b):
-        at = pl.multiple_of(b * tile, tile)
-        pltpu.make_async_copy(x_hbm.at[:, pl.ds(at, tile)], xv.at[b], loc_sem.at[0]).start()
-
+    early = [
+        pltpu.make_async_copy(src, dst, loc_sem.at[2 + k])
+        for k, (src, dst) in enumerate(
+            [
+                (cols_h, cols), (counts_h, counts), (tiles_h, tiles), (w1_h, w1), (cot_h, cot),
+                (w2_h, w2), (adj_h, adj), (b1_h, b1), (b2_h, b2),
+            ]
+        )
+    ]
+    for copy in early:
+        copy.start()
     barrier = pltpu.get_barrier_semaphore()
 
     @pl.loop(1, n)
@@ -76,6 +83,13 @@
             barrier, inc=1, device_id={"dp": lax.rem(my_dp + k, dp)}, device_id_type=pl.DeviceIdType.MESH
         )
 
+    @pl.loop(0, xv.shape[0])
+    def _(b):
+        at = pl.multiple_of(b * tile, tile)
+        pltpu.make_async_copy(x_hbm.at[:, pl.ds(at, tile)], xv.at[b], loc_sem.at[0]).start()
+
+    for copy in early:
+        copy.wait()
     count = counts[0, 0]
     lane = lax.broadcasted_iota(jnp.int32, (1, 128), 1)
     info = jnp.zeros((1, 128), jnp.int32)
@@ -374,7 +388,6 @@
     narrow = BF if rows % 16 == 0 else F32
     packed = slots * tile + 4 * sl
     vmem = pl.BlockSpec(memory_space=pltpu.VMEM)
-    smem = pl.BlockSpec(memory_space=pltpu.SMEM)
     dma = pltpu.SemaphoreType.DMA
     out2, gw1, gb1, gw2, gb2 = pl.pallas_call(
         functools.partial(kernel, n, dp, zs, xs),
@@ -385,9 +398,7 @@
             jax.ShapeDtypeStruct((2 * hid, hid), F32),
             jax.ShapeDtypeStruct((1, hid), F32),
         ),
-        in_specs=[
-            pl.BlockSpec(memory_space=pl.ANY), vmem, smem, smem, vmem, vmem, vmem, vmem, vmem, vmem,
-        ],
+        in_specs=[pl.BlockSpec(memory_space=pltpu.HBM)] * 10,
         out_specs=(vmem,) * 5,
         scratch_shapes=[
             pltpu.VMEM((width // tile, sl, tile), BF),
@@ -410,15 +421,24 @@
             pltpu.VMEM((dp, rows + 8, hid), F32),
             pltpu.VMEM((2 * sl, hid), BF),
             pltpu.VMEM((dp, 2 * sl, hid), BF),
+            pltpu.VMEM((slots, tile, tile), BF),
+            pltpu.SMEM((1, slots), jnp.int32),
+            pltpu.SMEM((1, 1), jnp.int32),
+            pltpu.VMEM((2, sl, hid), BF),
+            pltpu.VMEM((1, hid), F32),
+            pltpu.VMEM((tile, tile), BF),
+            pltpu.VMEM((2, hid, hid), BF),
+            pltpu.VMEM((1, hid), F32),
+            pltpu.VMEM((tile, hid), BF),
             dma((2, n, xs + 2)),
             dma((2, n)),
             dma((2, n, xs + 2)),
             dma((2, n)),
             dma((16,)),
-            dma((2,)),
+            dma((11,)),
         ],
         compiler_params=pltpu.CompilerParams(
-            collective_id=0, has_side_effects=True, vmem_limit_bytes=48 * 1024 * 1024
+            collective_id=0, has_side_effects=True, vmem_limit_bytes=63 * 1024 * 1024
         ),
     )(
         x_feat[0], tiles_one[0], tile_cols, tile_counts, w_one, b_one[None], adj_two[0], w_two,

time: 86.2 us -> 79.8 us (0.926)
  local copies, waits for them, and re-layouts: 11.5 us -> 7.36 us
  Pallas kernels: 73 us -> 70.8 us
    unnamed x23 -> x5, local copies, waits for them, and re-layouts: 11.5 us -> 7.36 us
    pallas_call x1, Pallas kernels: 73 us -> 70.8 us  [local(): pl.pallas_call(functools.partial(kernel, n, dp, zs, xs), out_shape=(jax.S...]
where the time goes in v2:
time: 79.8 us; the launch traced here: 79.5 us
  Pallas kernels  70.8 us (89%)
  local copies, waits for them, and re-layouts  7.36 us (9%)
  between operations  1.29 us (2%)
    pallas_call x1, Pallas kernels, local(): pl.pallas_call(functools.partial(kernel, n, dp, zs, xs), out_shape=(jax.S...  70.8 us
    unnamed x5, local copies, waits for them, and re-layouts  7.36 us

profile of v2, /device:TPU:0, one launch (start us, length us, event | category | flops | bytes accessed | tf_op | source)
XLA Modules:
  0.0 79.5 jit_solution(15545267511138480954)
XLA Ops:
  1.3 70.8 %shard_map.137 = (bf16[128,256]{1,0:T(8,128)(2,1)}, f32[128,256]{1,0:T(8,128)}, f32[1,256]{1,0:T(1,128)}, f32[512,256]{1,0:T(8,128)}, f32[1,256]{1,0:T(1,128)}) custom-call(bf16[64,26624]{1,0:T(8,128)(2,1)} %bitcast.11, bf16[4,128,128]{2,1,0:T(8,128)(2,1)} %bitcast.13, s32[1,4]{1,0:T(1,128)} %cols_h.1, s32[1,1]{1,0:T(1,128)S(6)} %copy.20.counts_h, ...), custom_call_target="tpu_custom_call" | custom-call | tf_op jit(solution)/shard_map/pallas_call | solution.py:392
  72.1 1.5 %copy.21 = bf16[1,128,256]{2,1,0:T(8,128)(2,1)} copy(bf16[1,128,256]{2,1,0:T(8,128)(2,1)} %bitcast.16) | data formatting | bytes 131072
  73.6 1.6 %copy.22 = f32[2,64,256]{2,1,0:T(8,128)} copy(f32[2,64,256]{2,1,0:T(8,128)} %bitcast.14) | data formatting | bytes 262144
  75.2 1.2 %copy.23 = f32[256]{0:T(256)} copy(f32[256]{0:T(256)} %bitcast.19) | data formatting | bytes 2048
  76.4 1.9 %copy.24 = f32[2,256,256]{2,1,0:T(8,128)} copy(f32[2,256,256]{2,1,0:T(8,128)} %bitcast.12) | data formatting | bytes 1048576
  78.3 1.2 %copy.25 = f32[256]{0:T(256)} copy(f32[256]{0:T(256)} %bitcast.18) | data formatting | bytes 2048

commit v3 on v2

--- a/solution.py
+++ b/solution.py
@@ -28,7 +28,7 @@
     x_hbm, tiles_h, cols_h, counts_h, w1_h, b1_h, adj_h, w2_h, b2_h, cot_h,
     out2, gw1, gb1, gw2, gb2,
     xv, pack, mv, agg, dzb, colv, coli, cols_s, dh_s, acc,
-    w2s, w2r, g2s, g2r, bs, bb, dps, dpr, w1s, w1r,
+    w2s, w2x, w2u, w2r, g2s, g2r, bs, bb, bt, br, dps, dpr, w1s, w1r,
     tiles, cols, counts, w1, b1, adj, w2, b2, cot,
     ag_send, ag_recv, dz_send, dz_recv, pair_sem, loc_sem,
 ):
@@ -44,7 +44,8 @@
     trows = slots * tile
     hid = w1.shape[2]
     half_w = hid // 2
-    rows = w2s.shape[1]
+    rows = w2s.shape[2]
+    half_n = n // 2
 
     def index(z, x, c):
         return (z * xs + x) * 2 + c
@@ -102,8 +103,10 @@
         for h in range(2):
             at = trows + (k * 2 + h) * sl
             pack[me, at : at + sl, :] = w1[k, :, h * half_w : (h + 1) * half_w]
-    bs[...] = jnp.zeros_like(bs)
-    bs[1:2, :] = jnp.sum(cot[...].astype(F32), axis=0, keepdims=True)
+    bs[:, hid:] = jnp.sum(cot[...].astype(F32), axis=0, keepdims=True)
+    dagg = dot(cot[...], w2[1], ((1,), (1,))).astype(BF)
+    dh = dot(cot[...], w2[0], ((1,), (1,)))
+    dh_s[...] = dh + dot(adj[...], dagg, ((0,), (0,)))
     pl.semaphore_wait(barrier, n - 1 + dp - 1)
 
     class Gather:
@@ -138,7 +141,13 @@
         def sibling(self, h, src, act):
             act(self.copy(h, src, xs + 1, index(zz, xx, 1 - core)))
 
-        def walk(self, act, first, arrive):
+        def walk(self, act, first, arrive, ready):
+            def from_sibling(z, x):
+                src = index(z, x, 1 - core)
+                arrive(0, src)
+                arrive(1, src)
+                ready(src)
+
             for h in (1, 0):
                 self.across(h, me, act)
                 self.up(h, me, act)
@@ -151,6 +160,7 @@
                 self.up(1, src, act)
                 self.down(1, src, act)
                 self.sibling(1, src, act)
+            ready(me)
 
             @pl.loop(1, zs)
             def _(k):
@@ -186,6 +196,22 @@
                         arrive(1, src)
                         self.down(1, src, act)
                         self.sibling(1, src, act)
+
+                @pl.when(zz - k >= 0)
+                def _():
+                    ready(index(zz - k, xx, core))
+
+                @pl.when(zz + k < zs)
+                def _():
+                    ready(index(zz + k, xx, core))
+
+                @pl.when(zz - k + 1 >= 0)
+                def _():
+                    from_sibling(zz - k + 1, xx)
+
+                @pl.when((zz + k - 1 < zs) & (k > 1))
+                def _():
+                    from_sibling(zz + k - 1, xx)
 
             @pl.loop(0, zs)
             def _(k):
@@ -194,31 +220,36 @@
                     src = index(z, lax.rem(xx + j, xs), core)
                     arrive(0, src)
                     self.sibling(0, src, act)
-
-        def run(self, first):
-            self.walk(lambda c: c.start(), first, self.wait)
+                    ready(src)
+
+            for z in ((zz - zs + 1), (zz + zs - 1)):
+                @pl.when((z >= 0) & (z < zs))
+                def _():
+                    from_sibling(z, xx)
+
+            @pl.loop(0, zs)
+            def _(k):
+                z = lax.rem(zz + k, zs)
+                for j in range(1, xs):
+                    from_sibling(z, lax.rem(xx + j, xs))
+
+        def run(self, first, ready):
+            self.walk(lambda c: c.start(), first, self.wait, ready)
 
         def finish(self):
-            self.walk(lambda c: c.wait_send(), lambda: None, lambda h, s: None)
-
-    def backward_start():
-        dagg = dot(cot[...], w2[1], ((1,), (1,))).astype(BF)
-        dh = dot(cot[...], w2[0], ((1,), (1,)))
-        dh_s[...] = dh + dot(adj[...], dagg, ((0,), (0,)))
+            self.walk(lambda c: c.wait_send(), lambda: None, lambda h, s: None, lambda s: None)
 
     def features_out():
-        wait_for(xv, loc_sem.at[0])
-
         @pl.loop(1, n)
         def _(k):
             p = lax.rem(me + k, n)
             remote(
-                xv.at[p], mv.at[0, me], pair_sem.at[2], pair_sem.at[3], p,
+                x_hbm.at[:, pl.ds(pl.multiple_of(p * tile, tile), tile)], mv.at[0, me],
+                pair_sem.at[2], pair_sem.at[3], p,
             ).start()
 
-        pltpu.make_async_copy(
-            xv.at[me], mv.at[0, me], pair_sem.at[3]
-        ).start()
+        at = pl.multiple_of(me * tile, tile)
+        pltpu.make_async_copy(x_hbm.at[:, pl.ds(at, tile)], mv.at[0, me], pair_sem.at[3]).start()
 
     @pl.loop(1, n)
     def _(k):
@@ -228,14 +259,13 @@
 
     def before_relay():
         features_out()
-        backward_start()
+        wait_for(coli, pair_sem.at[1])
+        to_smem = pltpu.make_async_copy(coli, cols_s, loc_sem.at[1])
+        to_smem.start()
+        to_smem.wait()
+        wait_for(xv, loc_sem.at[0])
 
     gather = Gather(pack, ag_send, ag_recv)
-    gather.run(before_relay)
-    wait_for(coli, pair_sem.at[1])
-    to_smem = pltpu.make_async_copy(coli, cols_s, loc_sem.at[1])
-    to_smem.start()
-    to_smem.wait()
 
     def aggregate(r):
         total = jnp.zeros((sl, tile), F32)
@@ -251,18 +281,7 @@
         def _():
             pltpu.make_async_copy(agg.at[r], mv.at[1, me], pair_sem.at[5]).start()
 
-    half_n = n // 2
-
-    @pl.loop(0, half_n)
-    def _(j):
-        aggregate(lax.rem(chip + j, half_n) * 2 + core)
-
-    @pl.loop(0, half_n)
-    def _(j):
-        r = lax.rem(chip + j, half_n) * 2 + 1 - core
-        gather.wait(0, r)
-        gather.wait(1, r)
-        aggregate(r)
+    gather.run(before_relay, aggregate)
 
     def project(k):
         at = trows + k * 2 * sl
@@ -283,33 +302,40 @@
     h_one = (z * sig).astype(BF)
     dz = (dh_s[...] * sig * (1.0 + z * (1.0 - sig))).astype(BF)
     dzb[me] = dz
-    bs[0:1, :] = jnp.sum(dz.astype(F32), axis=0, keepdims=True)
+    bs[:, :hid] = jnp.sum(dz.astype(F32), axis=0, keepdims=True)
 
     def forward():
         agg_two = dot(adj[...], h_one).astype(BF)
         g0 = dot(h_one, cot[...], ((0,), (0,)))
         g1 = dot(agg_two, cot[...], ((0,), (0,)))
-        w2s[: n // 2] = g0.reshape(n // 2, rows, hid).astype(w2s.dtype)
-        w2s[n // 2 :] = g1.reshape(n // 2, rows, hid).astype(w2s.dtype)
+        for j in range(n):
+            g = (g0, g1)[j // half_n]
+            at = (j % half_n) * rows
+            w2s[j % 2, j // 2] = g[at : at + rows].astype(w2s.dtype)
+        remote(w2s.at[1 - core], w2x, pair_sem.at[6], pair_sem.at[7], index(zz, xx, 1 - core)).start()
 
         @pl.loop(1, n)
         def _(k):
-            p = lax.rem(me + k, n)
-            remote(w2s.at[p], w2r.at[me], pair_sem.at[6], pair_sem.at[7], p).start()
-            remote(bs, bb.at[me], pair_sem.at[8], pair_sem.at[9], p).start()
-
-        pltpu.make_async_copy(w2s.at[me], w2r.at[me], pair_sem.at[7]).start()
+            remote(bs, bb.at[me], pair_sem.at[8], pair_sem.at[9], lax.rem(me + k, n)).start()
+
         pltpu.make_async_copy(bs, bb.at[me], pair_sem.at[9]).start()
         z2 = dot(h_one, w2[0]) + dot(agg_two, w2[1]) + b2[...]
         out2[...] = z2.astype(BF)
-
-    dgather = Gather(dzb, dz_send, dz_recv)
-    dgather.run(forward)
-
-    wait_for(w2r, pair_sem.at[7])
-    wait_for(bb, pair_sem.at[9])
-    dps[0:rows, :] = jnp.sum(w2r[...].astype(F32), axis=0)
-    dps[rows:, :] = jnp.sum(bb[...], axis=0)
+        wait_for(w2x, pair_sem.at[7])
+        w2u[...] = (w2s[core].astype(F32) + w2x[...].astype(F32)).astype(w2u.dtype)
+
+        @pl.loop(1, half_n)
+        def _(k):
+            p = lax.rem(chip + k, half_n)
+            remote(w2u.at[p], w2r.at[chip], pair_sem.at[10], pair_sem.at[11], p * 2 + core).start()
+
+        pltpu.make_async_copy(w2u.at[chip], w2r.at[chip], pair_sem.at[11]).start()
+
+    acc[...] = jnp.zeros_like(acc)
+
+    def weight(r):
+        lhs = jnp.concatenate([xv[r], agg[r]], axis=0)
+        acc[0 : 2 * sl, :] += dot(lhs, dzb[r])
 
     def over_replicas(src, dst, ssem, rsem):
         @pl.loop(1, dp)
@@ -318,64 +344,62 @@
 
         pltpu.make_async_copy(src, dst.at[my_dp], rsem).start()
 
-    over_replicas(dps, dpr, pair_sem.at[10], pair_sem.at[11])
-
-    acc[...] = jnp.zeros_like(acc)
-
-    def weight(r):
-        lhs = jnp.concatenate([xv[r], agg[r]], axis=0)
-        acc[0 : 2 * sl, :] += dot(lhs, dzb[r])
-
-    @pl.loop(0, half_n)
-    def _(j):
-        weight(lax.rem(chip + j, half_n) * 2 + core)
-
-    wait_for(dpr, pair_sem.at[11])
+    dgather = Gather(dzb, dz_send, dz_recv)
+    dgather.run(forward, weight)
+    w1s[...] = acc[0 : 2 * sl, :].astype(w1s.dtype)
+    over_replicas(w1s, w1r, pair_sem.at[14], pair_sem.at[15])
+
+    wait_for(w2r, pair_sem.at[11])
+    dps[...] = jnp.sum(w2r[...].astype(F32), axis=0)
+    over_replicas(dps, dpr, pair_sem.at[12], pair_sem.at[13])
+    wait_for(bb, pair_sem.at[9])
+    bt[...] = jnp.sum(bb[...], axis=0)
+    over_replicas(bt, br, pair_sem.at[16], pair_sem.at[17])
+    wait_for(dpr, pair_sem.at[13])
     total = dpr[0]
     for k in range(1, dp):
         total = total + dpr[k]
-    g2s[...] = total[0:rows].astype(g2s.dtype)
-    gb1[...] = total[rows : rows + 1]
-    gb2[...] = total[rows + 1 : rows + 2]
-
-    @pl.loop(1, n)
+    g2s[...] = total.astype(g2s.dtype)
+
+    @pl.loop(1, half_n)
     def _(k):
-        remote(g2s, g2r.at[me], pair_sem.at[12], pair_sem.at[13], lax.rem(me + k, n)).start()
-
-    pltpu.make_async_copy(g2s, g2r.at[me], pair_sem.at[13]).start()
-
-    @pl.loop(0, half_n)
-    def _(j):
-        r = lax.rem(chip + j, half_n) * 2 + 1 - core
-        dgather.wait(0, r)
-        dgather.wait(1, r)
-        weight(r)
-
-    w1s[...] = acc[0 : 2 * sl, :].astype(w1s.dtype)
-    over_replicas(w1s, w1r, pair_sem.at[14], pair_sem.at[15])
+        p = lax.rem(chip + k, half_n) * 2 + core
+        remote(g2s, g2r.at[core, chip], pair_sem.at[18], pair_sem.at[19], p).start()
+
+    pltpu.make_async_copy(g2s, g2r.at[core, chip], pair_sem.at[19]).start()
     gather.finish()
     dgather.finish()
-
-    def sent(ref, sem):
-        wait_for(ref, sem)
-
-    sent(coli.at[pl.ds(0, n - 1)], pair_sem.at[0])
-    sent(mv.at[0, pl.ds(0, n - 1)], pair_sem.at[2])
-    sent(mv.at[1, pl.ds(0, n - 1)], pair_sem.at[4])
-    sent(w2r.at[pl.ds(0, n - 1)], pair_sem.at[6])
-    sent(bb.at[pl.ds(0, n - 1)], pair_sem.at[8])
-    wait_for(g2r, pair_sem.at[13])
-    gw2[...] = g2r[...].astype(F32).reshape(n * rows, hid)
-    sent(g2r.at[pl.ds(0, n - 1)], pair_sem.at[12])
-    if dp > 1:
-        sent(dpr.at[pl.ds(0, dp - 1)], pair_sem.at[10])
+    wait_for(coli.at[pl.ds(0, n - 1)], pair_sem.at[0])
+    wait_for(mv.at[0, pl.ds(0, n - 1)], pair_sem.at[2])
+    wait_for(mv.at[1, pl.ds(0, n - 1)], pair_sem.at[4])
+    wait_for(w2x, pair_sem.at[6])
+    wait_for(bb.at[pl.ds(0, n - 1)], pair_sem.at[8])
+    wait_for(w2r.at[pl.ds(0, half_n - 1)], pair_sem.at[10])
+    wait_for(br, pair_sem.at[17])
+    bias = br[0]
+    for k in range(1, dp):
+        bias = bias + br[k]
+    gb1[...] = bias[:, :hid]
+    gb2[...] = bias[:, hid:]
     wait_for(w1r, pair_sem.at[15])
     total = w1r[0].astype(F32)
     for k in range(1, dp):
         total = total + w1r[k].astype(F32)
     gw1[...] = total
+    wait_for(g2r.at[core], pair_sem.at[19])
+    last = remote(
+        g2r.at[core], g2r.at[core], pair_sem.at[20], pair_sem.at[21], index(zz, xx, 1 - core)
+    )
+    last.start()
+    wait_for(g2r.at[1 - core], pair_sem.at[21])
+    for j in range(n):
+        gw2[j * rows : (j + 1) * rows] = g2r[j % 2, j // 2].astype(F32)
+    last.wait_send()
+    wait_for(g2r.at[0, pl.ds(0, half_n - 1)], pair_sem.at[18])
     if dp > 1:
-        sent(w1r.at[pl.ds(0, dp - 1)], pair_sem.at[14])
+        wait_for(dpr.at[pl.ds(0, dp - 1)], pair_sem.at[12])
+        wait_for(w1r.at[pl.ds(0, dp - 1)], pair_sem.at[14])
+        wait_for(br.at[pl.ds(0, dp - 1)], pair_sem.at[16])
 
 
 def local(n, dp, x_feat, tiles_one, tile_cols, tile_counts, w_one, b_one, adj_two, w_two, b_two, cotangent):
@@ -411,14 +435,18 @@
             pltpu.SMEM((n, 1, 128), jnp.int32),
             pltpu.VMEM((tile, hid), F32),
             pltpu.VMEM((max(tile, 2 * sl), hid), F32),
-            pltpu.VMEM((n, rows, hid), narrow),
-            pltpu.VMEM((n, rows, hid), narrow),
+            pltpu.VMEM((2, n // 2, rows, hid), narrow),
+            pltpu.VMEM((n // 2, rows, hid), narrow),
+            pltpu.VMEM((n // 2, rows, hid), narrow),
+            pltpu.VMEM((n // 2, rows, hid), narrow),
             pltpu.VMEM((rows, hid), narrow),
-            pltpu.VMEM((n, rows, hid), narrow),
-            pltpu.VMEM((8, hid), F32),
-            pltpu.VMEM((n, 8, hid), F32),
-            pltpu.VMEM((rows + 8, hid), F32),
-            pltpu.VMEM((dp, rows + 8, hid), F32),
+            pltpu.VMEM((2, n // 2, rows, hid), narrow),
+            pltpu.VMEM((1, 2 * hid), F32),
+            pltpu.VMEM((n, 1, 2 * hid), F32),
+            pltpu.VMEM((1, 2 * hid), F32),
+            pltpu.VMEM((dp, 1, 2 * hid), F32),
+            pltpu.VMEM((rows, hid), F32),
+            pltpu.VMEM((dp, rows, hid), F32),
             pltpu.VMEM((2 * sl, hid), BF),
             pltpu.VMEM((dp, 2 * sl, hid), BF),
             pltpu.VMEM((slots, tile, tile), BF),
@@ -434,7 +462,7 @@
             dma((2, n)),
             dma((2, n, xs + 2)),
             dma((2, n)),
-            dma((16,)),
+            dma((22,)),
             dma((11,)),
         ],
         compiler_params=pltpu.CompilerParams(

time: 79.8 us -> 78 us (0.977)
  Pallas kernels: 70.8 us -> 69 us
    pallas_call x1, Pallas kernels: 70.8 us -> 69 us  [local(): pl.pallas_call(functools.partial(kernel, n, dp, zs, xs), out_shape=(jax.S...]
where the time goes in v3:
time: 78 us; the launch traced here: 77.7 us
  Pallas kernels  69 us (88%)
  local copies, waits for them, and re-layouts  7.36 us (9%)
  between operations  1.29 us (2%)
    pallas_call x1, Pallas kernels, local(): pl.pallas_call(functools.partial(kernel, n, dp, zs, xs), out_shape=(jax.S...  69 us
    unnamed x5, local copies, waits for them, and re-layouts  7.36 us

profile of v3, /device:TPU:0, one launch (start us, length us, event | category | flops | bytes accessed | tf_op | source)
XLA Modules:
  0.0 77.7 jit_solution(4553976653205914984)
XLA Ops:
  1.3 69.0 %shard_map.137 = (bf16[128,256]{1,0:T(8,128)(2,1)}, f32[128,256]{1,0:T(8,128)}, f32[1,256]{1,0:T(1,128)}, f32[512,256]{1,0:T(8,128)}, f32[1,256]{1,0:T(1,128)}) custom-call(bf16[64,26624]{1,0:T(8,128)(2,1)} %bitcast.11, bf16[4,128,128]{2,1,0:T(8,128)(2,1)} %bitcast.13, s32[1,4]{1,0:T(1,128)} %cols_h.1, s32[1,1]{1,0:T(1,128)S(6)} %copy.20.counts_h, ...), custom_call_target="tpu_custom_call" | custom-call | tf_op jit(solution)/shard_map/pallas_call | solution.py:416
  70.3 1.5 %copy.21 = bf16[1,128,256]{2,1,0:T(8,128)(2,1)} copy(bf16[1,128,256]{2,1,0:T(8,128)(2,1)} %bitcast.16) | data formatting | bytes 131072
  71.8 1.6 %copy.22 = f32[2,64,256]{2,1,0:T(8,128)} copy(f32[2,64,256]{2,1,0:T(8,128)} %bitcast.14) | data formatting | bytes 262144
  73.4 1.2 %copy.23 = f32[256]{0:T(256)} copy(f32[256]{0:T(256)} %bitcast.19) | data formatting | bytes 2048
  74.6 1.9 %copy.24 = f32[2,256,256]{2,1,0:T(8,128)} copy(f32[2,256,256]{2,1,0:T(8,128)} %bitcast.12) | data formatting | bytes 1048576
  76.5 1.2 %copy.25 = f32[256]{0:T(256)} copy(f32[256]{0:T(256)} %bitcast.18) | data formatting | bytes 2048

commit v4 on v3

--- a/solution.py
+++ b/solution.py
@@ -103,10 +103,6 @@
         for h in range(2):
             at = trows + (k * 2 + h) * sl
             pack[me, at : at + sl, :] = w1[k, :, h * half_w : (h + 1) * half_w]
-    bs[:, hid:] = jnp.sum(cot[...].astype(F32), axis=0, keepdims=True)
-    dagg = dot(cot[...], w2[1], ((1,), (1,))).astype(BF)
-    dh = dot(cot[...], w2[0], ((1,), (1,)))
-    dh_s[...] = dh + dot(adj[...], dagg, ((0,), (0,)))
     pl.semaphore_wait(barrier, n - 1 + dp - 1)
 
     class Gather:
@@ -141,7 +137,7 @@
         def sibling(self, h, src, act):
             act(self.copy(h, src, xs + 1, index(zz, xx, 1 - core)))
 
-        def walk(self, act, first, arrive, ready):
+        def walk(self, act, first, arrive, ready, middle=lambda: None, late=lambda: None):
             def from_sibling(z, x):
                 src = index(z, x, 1 - core)
                 arrive(0, src)
@@ -213,6 +209,8 @@
                 def _():
                     from_sibling(zz + k - 1, xx)
 
+            middle()
+
             @pl.loop(0, zs)
             def _(k):
                 z = lax.rem(zz + k, zs)
@@ -222,6 +220,7 @@
                     self.sibling(0, src, act)
                     ready(src)
 
+            late()
             for z in ((zz - zs + 1), (zz + zs - 1)):
                 @pl.when((z >= 0) & (z < zs))
                 def _():
@@ -233,8 +232,8 @@
                 for j in range(1, xs):
                     from_sibling(z, lax.rem(xx + j, xs))
 
-        def run(self, first, ready):
-            self.walk(lambda c: c.start(), first, self.wait, ready)
+        def run(self, first, ready, *between):
+            self.walk(lambda c: c.start(), first, self.wait, ready, *between)
 
         def finish(self):
             self.walk(lambda c: c.wait_send(), lambda: None, lambda h, s: None, lambda s: None)
@@ -259,6 +258,10 @@
 
     def before_relay():
         features_out()
+        bs[:, hid:] = jnp.sum(cot[...].astype(F32), axis=0, keepdims=True)
+        dagg = dot(cot[...], w2[1], ((1,), (1,))).astype(BF)
+        dh = dot(cot[...], w2[0], ((1,), (1,)))
+        dh_s[...] = dh + dot(adj[...], dagg, ((0,), (0,)))
         wait_for(coli, pair_sem.at[1])
         to_smem = pltpu.make_async_copy(coli, cols_s, loc_sem.at[1])
         to_smem.start()
@@ -344,29 +347,33 @@
 
         pltpu.make_async_copy(src, dst.at[my_dp], rsem).start()
 
+    def middle():
+        wait_for(w2r, pair_sem.at[11])
+        dps[...] = jnp.sum(w2r[...].astype(F32), axis=0)
+        over_replicas(dps, dpr, pair_sem.at[12], pair_sem.at[13])
+        wait_for(bb, pair_sem.at[9])
+        bt[...] = jnp.sum(bb[...], axis=0)
+        over_replicas(bt, br, pair_sem.at[16], pair_sem.at[17])
+
+    def late():
+        wait_for(dpr, pair_sem.at[13])
+        total = dpr[0]
+        for k in range(1, dp):
+            total = total + dpr[k]
+        g2s[...] = total.astype(g2s.dtype)
+
+        @pl.loop(1, half_n)
+        def _(k):
+            p = lax.rem(chip + k, half_n) * 2 + core
+            remote(g2s, g2r.at[core, chip], pair_sem.at[18], pair_sem.at[19], p).start()
+
+        pltpu.make_async_copy(g2s, g2r.at[core, chip], pair_sem.at[19]).start()
+
     dgather = Gather(dzb, dz_send, dz_recv)
-    dgather.run(forward, weight)
+    dgather.run(forward, weight, middle, late)
     w1s[...] = acc[0 : 2 * sl, :].astype(w1s.dtype)
     over_replicas(w1s, w1r, pair_sem.at[14], pair_sem.at[15])
 
-    wait_for(w2r, pair_sem.at[11])
-    dps[...] = jnp.sum(w2r[...].astype(F32), axis=0)
-    over_replicas(dps, dpr, pair_sem.at[12], pair_sem.at[13])
-    wait_for(bb, pair_sem.at[9])
-    bt[...] = jnp.sum(bb[...], axis=0)
-    over_replicas(bt, br, pair_sem.at[16], pair_sem.at[17])
-    wait_for(dpr, pair_sem.at[13])
-    total = dpr[0]
-    for k in range(1, dp):
-        total = total + dpr[k]
-    g2s[...] = total.astype(g2s.dtype)
-
-    @pl.loop(1, half_n)
-    def _(k):
-        p = lax.rem(chip + k, half_n) * 2 + core
-        remote(g2s, g2r.at[core, chip], pair_sem.at[18], pair_sem.at[19], p).start()
-
-    pltpu.make_async_copy(g2s, g2r.at[core, chip], pair_sem.at[19]).start()
     gather.finish()
     dgather.finish()
     wait_for(coli.at[pl.ds(0, n - 1)], pair_sem.at[0])
@@ -402,6 +409,16 @@
         wait_for(br.at[pl.ds(0, dp - 1)], pair_sem.at[16])
 
 
+def hand_over(*refs):
+    count = len(refs) // 2
+    sems = refs[-1]
+    copies = [pltpu.make_async_copy(refs[k], refs[count + k], sems.at[k]) for k in range(count)]
+    for copy in copies:
+        copy.start()
+    for copy in copies:
+        copy.wait()
+
+
 def local(n, dp, x_feat, tiles_one, tile_cols, tile_counts, w_one, b_one, adj_two, w_two, b_two, cotangent):
     zs, xs = grid_of(n)
     sl, width = x_feat.shape[1:]
@@ -413,7 +430,7 @@
     packed = slots * tile + 4 * sl
     vmem = pl.BlockSpec(memory_space=pltpu.VMEM)
     dma = pltpu.SemaphoreType.DMA
-    out2, gw1, gb1, gw2, gb2 = pl.pallas_call(
+    results = pl.pallas_call(
         functools.partial(kernel, n, dp, zs, xs),
         out_shape=(
             jax.ShapeDtypeStruct((tile, hid), BF),
@@ -472,6 +489,15 @@
         x_feat[0], tiles_one[0], tile_cols, tile_counts, w_one, b_one[None], adj_two[0], w_two,
         b_two[None], cotangent[0],
     )
+    anywhere = pl.BlockSpec(memory_space=pl.ANY)
+    out2, gw1, gb1, gw2, gb2 = pl.pallas_call(
+        hand_over,
+        out_shape=tuple(jax.ShapeDtypeStruct(r.shape, r.dtype) for r in results),
+        in_specs=[anywhere] * 5,
+        out_specs=(anywhere,) * 5,
+        scratch_shapes=[dma((5,))],
+        compiler_params=pltpu.CompilerParams(vmem_limit_bytes=63 * 1024 * 1024),
+    )(*results)
     return (
         out2[None], gw1.reshape(2, sl, hid), gb1[0], gw2.reshape(2, hid, hid), gb2[0],
     )

time: 78 us -> 89 us (1.14)
  Pallas kernels: 69 us -> 87.5 us
  local copies, waits for them, and re-layouts: 7.36 us -> 0 us
    pallas_call x0 -> x1, Pallas kernels: none -> 23 us  [local(): pl.pallas_call(hand_over, out_shape=tuple((jax.ShapeDtypeStruct(r.shape,...]
    unnamed x5 -> x0, local copies, waits for them, and re-layouts: 7.36 us -> none
    pallas_call x1, Pallas kernels: 69 us -> 64.5 us  [local(): pl.pallas_call(functools.partial(kernel, n, dp, zs, xs), out_shape=(jax.S...]
where the time goes in v4:
time: 89 us; the launch traced here: 88.8 us
  Pallas kernels  87.5 us (98%)
  between operations  1.29 us (1%)
    pallas_call x1, Pallas kernels, local(): pl.pallas_call(functools.partial(kernel, n, dp, zs, xs), out_shape=(jax.S...  64.5 us
    pallas_call x1, Pallas kernels, local(): pl.pallas_call(hand_over, out_shape=tuple((jax.ShapeDtypeStruct(r.shape,...  23 us

profile of v4, /device:TPU:0, one launch (start us, length us, event | category | flops | bytes accessed | tf_op | source)
XLA Modules:
  0.0 88.8 jit_solution(17374084377012151482)
XLA Ops:
  1.3 64.5 %shard_map.137 = (bf16[128,256]{1,0:T(8,128)(2,1)}, f32[128,256]{1,0:T(8,128)}, f32[1,256]{1,0:T(1,128)}, f32[512,256]{1,0:T(8,128)}, f32[1,256]{1,0:T(1,128)}) custom-call(bf16[64,26624]{1,0:T(8,128)(2,1)} %bitcast.11, bf16[4,128,128]{2,1,0:T(8,128)(2,1)} %bitcast.12, s32[1,4]{1,0:T(1,128)} %cols_h.1, s32[1,1]{1,0:T(1,128)S(6)} %copy.15.counts_h, ...), custom_call_target="tpu_custom_call" | custom-call | tf_op jit(solution)/shard_map/pallas_call | solution.py:433
  65.8 23.0 %shard_map.138 = (bf16[128,256]{1,0:T(8,128)(2,1)}, f32[128,256]{1,0:T(8,128)}, f32[1,256]{1,0:T(1,128)}, f32[512,256]{1,0:T(8,128)}, f32[1,256]{1,0:T(1,128)}) custom-call(bf16[128,256]{1,0:T(8,128)(2,1)} %get-tuple-element.15.refs_0_, f32[128,256]{1,0:T(8,128)} %get-tuple-element.16.refs_1_, f32[1,256]{1,0:T(1,128)} %get-tuple-element.17.refs_2_, ...), custom_call_target="tpu_custom_call" | custom-call | tf_op jit(solution)/shard_map/pallas_call | solution.py:493

commit v5 on v4

--- a/solution.py
+++ b/solution.py
@@ -409,16 +409,6 @@
         wait_for(br.at[pl.ds(0, dp - 1)], pair_sem.at[16])
 
 
-def hand_over(*refs):
-    count = len(refs) // 2
-    sems = refs[-1]
-    copies = [pltpu.make_async_copy(refs[k], refs[count + k], sems.at[k]) for k in range(count)]
-    for copy in copies:
-        copy.start()
-    for copy in copies:
-        copy.wait()
-
-
 def local(n, dp, x_feat, tiles_one, tile_cols, tile_counts, w_one, b_one, adj_two, w_two, b_two, cotangent):
     zs, xs = grid_of(n)
     sl, width = x_feat.shape[1:]
@@ -430,7 +420,7 @@
     packed = slots * tile + 4 * sl
     vmem = pl.BlockSpec(memory_space=pltpu.VMEM)
     dma = pltpu.SemaphoreType.DMA
-    results = pl.pallas_call(
+    out2, gw1, gb1, gw2, gb2 = pl.pallas_call(
         functools.partial(kernel, n, dp, zs, xs),
         out_shape=(
             jax.ShapeDtypeStruct((tile, hid), BF),
@@ -489,15 +479,6 @@
         x_feat[0], tiles_one[0], tile_cols, tile_counts, w_one, b_one[None], adj_two[0], w_two,
         b_two[None], cotangent[0],
     )
-    anywhere = pl.BlockSpec(memory_space=pl.ANY)
-    out2, gw1, gb1, gw2, gb2 = pl.pallas_call(
-        hand_over,
-        out_shape=tuple(jax.ShapeDtypeStruct(r.shape, r.dtype) for r in results),
-        in_specs=[anywhere] * 5,
-        out_specs=(anywhere,) * 5,
-        scratch_shapes=[dma((5,))],
-        compiler_params=pltpu.CompilerParams(vmem_limit_bytes=63 * 1024 * 1024),
-    )(*results)
     return (
         out2[None], gw1.reshape(2, sl, hid), gb1[0], gw2.reshape(2, hid, hid), gb2[0],
     )

time: 89 us -> 73.4 us (0.82)
  Pallas kernels: 87.5 us -> 64.5 us
  local copies, waits for them, and re-layouts: 0 us -> 7.36 us
    pallas_call x1 -> x0, Pallas kernels: 23 us -> none  [local(): pl.pallas_call(hand_over, out_shape=tuple((jax.ShapeDtypeStruct(r.shape,...]
    unnamed x0 -> x5, local copies, waits for them, and re-layouts: none -> 7.36 us
where the time goes in v5:
time: 73.4 us; the launch traced here: 73.1 us
  Pallas kernels  64.5 us (88%)
  local copies, waits for them, and re-layouts  7.36 us (10%)
  between operations  1.29 us (2%)
    pallas_call x1, Pallas kernels, local(): pl.pallas_call(functools.partial(kernel, n, dp, zs, xs), out_shape=(jax.S...  64.5 us
    unnamed x5, local copies, waits for them, and re-layouts  7.36 us

profile of v5, /device:TPU:0, one launch (start us, length us, event | category | flops | bytes accessed | tf_op | source)
XLA Modules:
  0.0 73.1 jit_solution(9755714738033849143)
XLA Ops:
  1.3 64.5 %shard_map.137 = (bf16[128,256]{1,0:T(8,128)(2,1)}, f32[128,256]{1,0:T(8,128)}, f32[1,256]{1,0:T(1,128)}, f32[512,256]{1,0:T(8,128)}, f32[1,256]{1,0:T(1,128)}) custom-call(bf16[64,26624]{1,0:T(8,128)(2,1)} %bitcast.11, bf16[4,128,128]{2,1,0:T(8,128)(2,1)} %bitcast.13, s32[1,4]{1,0:T(1,128)} %cols_h.1, s32[1,1]{1,0:T(1,128)S(6)} %copy.20.counts_h, ...), custom_call_target="tpu_custom_call" | custom-call | tf_op jit(solution)/shard_map/pallas_call | solution.py:423
  65.8 1.5 %copy.21 = bf16[1,128,256]{2,1,0:T(8,128)(2,1)} copy(bf16[1,128,256]{2,1,0:T(8,128)(2,1)} %bitcast.16) | data formatting | bytes 131072
  67.2 1.6 %copy.22 = f32[2,64,256]{2,1,0:T(8,128)} copy(f32[2,64,256]{2,1,0:T(8,128)} %bitcast.14) | data formatting | bytes 262144
  68.8 1.2 %copy.23 = f32[256]{0:T(256)} copy(f32[256]{0:T(256)} %bitcast.19) | data formatting | bytes 2048
  70.0 1.9 %copy.24 = f32[2,256,256]{2,1,0:T(8,128)} copy(f32[2,256,256]{2,1,0:T(8,128)} %bitcast.12) | data formatting | bytes 1048576
  71.9 1.2 %copy.25 = f32[256]{0:T(256)} copy(f32[256]{0:T(256)} %bitcast.18) | data formatting | bytes 2048
